TPU v7x, 128 devices: a whole 4x4x4 slice. The times are simulated.
128 devices in a mesh: grid: 4 (over x), blk: 32 (over z, y, core).
Axes of the slice: x: 4, y: 4, z: 4, core: 2. Of those that a mesh axis runs over, the one named last changes fastest.
Arguments:
- state: float32 [4, 4, 128, 128, 128], P('grid', None, 'blk'), may hold values from -6 to 6
- metric: float32 [4, 9, 128, 128, 128], P('grid', None, 'blk'), may hold values from -3 to 3
- damping: float32 [4, 128, 128, 128], P('grid', 'blk'), may hold values from 0 to 1.5
- donor: int32 [4, 131072], P('grid', 'blk'), may hold values from 16384 to 81790, as said below
- fractions: float32 [4, 3, 131072], P('grid', None, 'blk'), may hold values from 0 to 1
- dest: int32 [4, 131072, 1], P('grid', 'blk'), may hold values from 0 to 127; in each aligned block of 4096 rows (0 to 4095, 4096 to 8191, ..., all dimensions but the last counted through in order) at most 64 rows name the same one
- recept: int32 [4, 131072], P('grid', 'blk'), may hold values from 0 to 65535
Outputs:
- updated: float32 [4, 4, 128, 128, 128], P('grid', None, 'blk')
Inputs may be any that keep to these rules, and one draw needn't show every extreme that they name: A flat index a * 128 * 128 + c * 128 + e into the donor's block extended by one cell at both ends of the first dimension, with a from 1 to 4 (to 3 on the last block of each grid), c below 127 and e below 127. `dest`: among the rows of one device, at most 64 name the same receiving block. `recept`: a cell of the receiving block, flat over its three dimensions.
All inputs are finite; a program needn't handle non-finite values.
Results may differ from a plain program's by a relative error of at most 0.00002.
Values sent between devices are 32-bit elements; how exact they have to be, the bound alone decides.
No kernel may reach another device: no remote copies, remote signals or barrier semaphores. Data moves between devices by JAX's collectives and lax.ppermute only.
A program may use at most 192 MiB of HBM per device.

v0:
```python
import functools
import jax
import jax.numpy as jnp
from jax import lax
from jax.experimental import pallas as pl
from jax.experimental.pallas import tpu as pltpu
from jax.sharding import PartitionSpec as P

step_size = 0.4
f32, bf16, i32 = jnp.float32, jnp.bfloat16, jnp.int32
VMEM_LIMIT = 40 * 1024 * 1024
NT = (((1,), (1,)), ((), ()))


def iota(shape, dim):
    return lax.broadcasted_iota(i32, shape, dim)


def two_parts(x):
    high = x.astype(bf16)
    low = (x - high.astype(f32)).astype(bf16)
    return high, low


def params(limit=VMEM_LIMIT):
    return pltpu.CompilerParams(vmem_limit_bytes=limit)


TILE = 256
NEAR_GROUP = 8
FAR_GROUP = 5
WHOLE_GROUP = 10
DONOR_ROWS = 24
RANKS = 16


def placed(kinds):
    spaces = {"v": pltpu.VMEM, "s": pltpu.SMEM, "h": pltpu.HBM}
    return [pl.BlockSpec(memory_space=spaces[kind]) for kind in kinds]


def exact(mask):
    return mask.astype(f32).astype(bf16)


def starts_of(counts):
    tiles = [(count + TILE - 1) // TILE for count in counts]
    first = tiles[0]
    second = first + tiles[1]
    third = second + tiles[2]
    return first, second, third, third + tiles[3]


def prepare_kernel(numbers, fractions, table, labels, starts):
    donor, dest, recept = numbers.at[0], numbers.at[1], numbers.at[2]
    chunks = [slice(i, i + TILE) for i in range(0, donor.shape[1], TILE)]
    plane_all = donor[...] >> 14
    counts = [jnp.sum((plane_all == p + 1).astype(f32)).astype(i32) for p in range(4)]
    begin = starts_of(counts)
    for i in range(4):
        starts[i] = begin[i]
    offsets = (0,) + begin[:3]
    blocks = iota((144, TILE), 0)
    slots = iota((64, TILE), 0)
    high_rows = iota((DONOR_ROWS, TILE), 0)
    low_rows = iota((TILE, TILE), 0)
    before = exact(iota((TILE, TILE), 0) < iota((TILE, TILE), 1))
    blank = jnp.zeros((8, TILE), f32)

    members = []
    for here in chunks:
        member = (blocks == dest[:, here]) | (blocks == (donor[:, here] >> 14) + 127)
        amount = jnp.where((blocks < 128) & (recept[:, here] >= 32768), 128.0, 1.0)
        members.append(jnp.where(member, amount, 0.0))
    earlier = jnp.dot(jnp.concatenate(members, axis=0).astype(bf16), before, preferred_element_type=f32)
    counted = jnp.zeros((144, 1), f32)
    spreads, places, targets, marks = [], [], [], []
    for i, here in enumerate(chunks):
        inside = members[i] > 0.0
        ranked = jnp.where(inside, earlier[i * 144 : i * 144 + 144] + counted, 0.0)
        counted = counted + jnp.sum(members[i], axis=1, keepdims=True)
        rank = jnp.sum(ranked[:128], axis=0, keepdims=True).astype(i32)
        spot = jnp.sum(ranked[128:], axis=0, keepdims=True).astype(i32)
        label = recept[:, here]
        rank = jnp.where(label >= 32768, 63 - (rank >> 7), rank & 127)
        base = donor[:, here]
        plane = base >> 14
        offset = jnp.where(plane == 1, offsets[0], jnp.where(plane == 2, offsets[1], jnp.where(plane == 3, offsets[2], offsets[3])))
        chosen = high_rows == offset + (spot >> 8)
        fields = [(base >> 7) & 127, base & 127, dest[:, here], rank + 1]
        fields = [field.astype(f32) for field in fields]
        for k in range(3):
            rest = fractions[k, :, here]
            for _ in range(3):
                part = rest.astype(bf16).astype(f32)
                fields.append(part)
                rest = rest - part
        spread = jnp.concatenate([jnp.where(chosen, field, 0.0) for field in fields] + [blank], axis=0)
        spreads.append(spread.astype(bf16))
        places.append(exact(low_rows == (spot & 255)))
        held = slots == rank
        mark = [jnp.where(held, part.astype(f32), 0.0) for part in ((label + 1) >> 8, (label + 1) & 255)]
        marks.append(jnp.concatenate(mark, axis=0).astype(bf16))
        targets.append(exact(inside[:128]))

    def gathered(left, right):
        left, right = jnp.concatenate(left, axis=1), jnp.concatenate(right, axis=1)
        return lax.dot_general(left, right, NT, preferred_element_type=f32)

    both = gathered(targets, marks) * jnp.where(iota((128, 128), 1) < 64, 256.0, 1.0)
    labels[...] = both + pltpu.roll(both, 64, 1)
    total = gathered(spreads, places)

    def field(i):
        return total[i * DONOR_ROWS : (i + 1) * DONOR_ROWS]

    for i in range(4):
        table[i] = field(i)
    for i in range(3):
        table[4 + i] = field(4 + 3 * i) + field(5 + 3 * i) + field(6 + 3 * i)


def prepare(donor, fractions, dest, recept):
    numbers = jnp.concatenate([x.reshape(1, 1, -1) for x in (donor, dest, recept)], axis=0)
    return pl.pallas_call(
        prepare_kernel,
        out_shape=(
            jax.ShapeDtypeStruct((7, DONOR_ROWS, TILE), f32),
            jax.ShapeDtypeStruct((128, 128), f32),
            jax.ShapeDtypeStruct((4,), i32),
        ),
        in_specs=placed("vv"),
        out_specs=tuple(placed("vvs")),
        compiler_params=params(),
        cost_estimate=pl.CostEstimate(flops=3 * 10**9, bytes_accessed=10**6, transcendentals=0),
    )(numbers, fractions)


def pack_kernel(far, with_labels, *refs):
    if far:
        fetched, _, beyond, table, starts, given, out, source, total, state, sems = refs
        held = fetched if with_labels else fetched.at[:, 3:4]
        copies = [pltpu.make_async_copy(held.at[c], state.at[c], sems.at[c]) for c in range(4)]
    else:
        fetched, table, starts, total, source, state, sems = refs
        copies = [pltpu.make_async_copy(fetched.at[c], state.at[c], sems.at[c]) for c in range(4)]
    for copy in copies:
        copy.start()
    inner = lax.axis_index("blk") < lax.axis_size("blk") - 1
    planes = state.shape[1]
    for c in range(4):
        copies[c].wait()
        rows = slice(c * 128, c * 128 + 128)
        for x in range(planes + far):
            high, low = two_parts(state[c, x] if x < planes else jnp.where(inner, beyond[c], 0.0))
            source[0, rows, x * 128 : x * 128 + 128] = high
            source[1, rows, x * 128 : x * 128 + 128] = low
    total[...] = given[...] if far and not with_labels else jnp.zeros_like(total)
    cells = iota((128, TILE), 0)
    slots = iota((64, TILE), 0)
    first = starts[2] if far and not with_labels else 0
    last = starts[3] if far else starts[2]
    group = WHOLE_GROUP if with_labels else FAR_GROUP if far else NEAR_GROUP
    inside = 3 if with_labels else 0 if far else 2

    def interpolated(t):
        line, point, target, rank, fx, fy, fz = (table[i, pl.ds(t, 1), :] for i in range(7))
        line, point, target, rank = (v.astype(i32) for v in (line, point, target, rank))
        wy = jnp.where(cells == line, 1.0 - fy, jnp.where(cells == line + 1, fy, 0.0))
        wz = jnp.where(cells == point, 1.0 - fz, jnp.where(cells == point + 1, fz, 0.0))
        lower, upper = two_parts(wz * (1.0 - fx)), two_parts(wz * fx)
        high = [lower[0], upper[0]]
        weights = jnp.concatenate(high + high + [lower[1], upper[1]], axis=0)
        pair = sum((t >= starts[i]).astype(i32) for i in range(inside))
        both = pl.ds(pl.multiple_of(pair * 128, 128), 256) if inside else slice(0, 256)
        high, low = source[0, :, both], source[1, :, both]
        lines = jnp.dot(jnp.concatenate([high, low, high], axis=1), weights, preferred_element_type=f32)
        chosen = slots == jnp.where(t < last, rank - 1, -1)
        values = [jnp.sum(lines[c * 128 : c * 128 + 128] * wy, axis=0, keepdims=True) for c in range(4)]
        parts = []
        for which in (0, 1):
            for c in range(4):
                part = two_parts(values[c])[which].astype(f32)
                parts.append(jnp.where(chosen, part, 0.0).astype(bf16))
        return exact(cells == target), jnp.concatenate(parts, axis=0)

    def step(t, _):
        members, packed = zip(*[interpolated(first + t * group + j) for j in range(group)])
        members, packed = jnp.concatenate(members, axis=1), jnp.concatenate(packed, axis=1)
        total[...] += lax.dot_general(members, packed, NT, preferred_element_type=f32)
        return 0

    lax.fori_loop(0, (last - first + group - 1) // group, step, 0)
    if not far:
        return
    for half in range(2):
        cut = slice(half * 128, half * 128 + 128)
        low = slice(256 + half * 128, 256 + half * 128 + 128)
        out[:, 0, cut] = total[:, cut] + total[:, low]
    if with_labels:
        out[:, 0, 256:384] = given[...]


def pack_near(state, table, starts):
    return pl.pallas_call(
        functools.partial(pack_kernel, 0, False),
        out_shape=jax.ShapeDtypeStruct((128, 512), f32),
        in_specs=placed("hvs"),
        out_specs=placed("v")[0],
        scratch_shapes=[
            pltpu.VMEM((2, 512, 512), bf16),
            pltpu.VMEM(state.shape, f32),
            pltpu.SemaphoreType.DMA((4,)),
        ],
        compiler_params=params(),
        cost_estimate=pl.CostEstimate(flops=5 * 10**9, bytes_accessed=10**6, transcendentals=0),
    )(state, table, starts)


def pack_rest(first, state, below, beyond, table, starts, given):
    planes = 4 if first else 1
    return pl.pallas_call(
        functools.partial(pack_kernel, 1, first),
        out_shape=jax.ShapeDtypeStruct((128, 1, 384 if first else 256), f32),
        in_specs=placed("hhvvsv"),
        out_specs=placed("v")[0],
        scratch_shapes=[
            pltpu.VMEM((2, 512, planes * 128 + 128), bf16),
            pltpu.VMEM((128, 512), f32),
            pltpu.VMEM((4, planes, 128, 128), f32),
            pltpu.SemaphoreType.DMA((4,)),
        ],
        compiler_params=params(),
    )(state, below, beyond, table, starts, given)


def rates_of(x, state, below, beyond, metric, damping):
    row = iota((128, 128), 0)
    lane = iota((128, 128), 1)

    block = lax.axis_index("blk")
    inner = block > 0, block < lax.axis_size("blk") - 1

    def differences(c):
        here = state[c, x]
        low = jnp.where(inner[0], below[c], 0.0) if x == 0 else state[c, x - 1]
        high = jnp.where(inner[1], beyond[c], 0.0) if x == 3 else state[c, x + 1]
        up = jnp.where(row < 127, pltpu.roll(here, 127, 0), 0.0)
        down = jnp.where(row > 0, pltpu.roll(here, 1, 0), 0.0)
        right = jnp.where(lane < 127, pltpu.roll(here, 127, 1), 0.0)
        left = jnp.where(lane > 0, pltpu.roll(here, 1, 1), 0.0)
        return (high - low) * 0.5, (up - down) * 0.5, (right - left) * 0.5

    def gradient(diffs, i):
        return metric[i, x] * diffs[0] + metric[3 + i, x] * diffs[1] + metric[6 + i, x] * diffs[2]

    damp = damping[x]
    pressure = -damp * state[0, x]
    for i in range(3):
        pressure = pressure - gradient(differences(1 + i), i)
    diffs = differences(0)
    return [pressure] + [-gradient(diffs, i) - damp * state[1 + i, x] for i in range(3)]


def deposit_kernel(first, *refs):
    fetches = 5 if first else 6
    arrived, fetched, refs = refs[0], refs[1 : fetches + 1], refs[fetches + 1 :]
    if first:
        low_plane, high_plane, out, counts, cells, bounds, *scratch = refs
    else:
        counts, cells, bounds, out, *scratch = refs
    slots, total, count, sems, *held = scratch
    now, below, beyond, metric, damping = held[:5]
    copies = [pltpu.make_async_copy(fetched[i], held[i], sems.at[i]) for i in range(fetches)]
    for copy in copies:
        copy.start()
    for j in range(2):
        turned = arrived[:, 0, j * 128 : j * 128 + 128].T
        for half in range(2):
            high, low = two_parts(turned[half * 64 : half * 64 + 64])
            slots[2 * j + half] = high.astype(f32)
            slots[4 + 2 * j + half] = low.astype(f32)
    if first:
        label = arrived[:, 0, 256:384].T[:64].astype(i32) - 1
        cells[0] = (label >> 7) & 127
        cells[1] = (label >> 14) * 128 + (label & 127)
        rank = iota((64, 128), 0)
        front = (label >= 0) & (label < 32768)
        bounds[0] = (jnp.max(jnp.where(front, rank + 1, 0).astype(f32)).astype(i32) + RANKS - 1) // RANKS
        bounds[1] = jnp.min(jnp.where(label >= 32768, rank, 64).astype(f32)).astype(i32) // RANKS
        count[...] = jnp.zeros_like(count)
    total[...] = jnp.zeros_like(total)
    lines = iota((128, 128), 0)
    points = iota((256, 128), 0)

    def add(pairs, t, _):
        high, low, ones, selectors = [], [], [], []
        for j in range(RANKS):
            row = pl.ds(t * RANKS + j, 1)
            at = lines == cells[0, row, :]

            def spread(f):
                return jnp.where(at, slots[f, row, :], 0.0).astype(bf16)

            high.append(jnp.concatenate([spread(f) for f in range(4)], axis=0))
            low.append(jnp.concatenate([spread(4 + f) for f in range(4)], axis=0))
            ones.append(exact(at))
            point = cells[1, row, :]
            selectors.append(jnp.concatenate([exact(points == point - 256 * p) for p in pairs], axis=0))
        selector = jnp.concatenate(selectors + selectors, axis=1)
        added = lax.dot_general(jnp.concatenate(high + low, axis=1), selector, NT, preferred_element_type=f32)
        for i, p in enumerate(pairs):
            total[p] += added[:, i * 256 : i * 256 + 256]
        if first:
            selector = jnp.concatenate(selectors, axis=1)
            added = lax.dot_general(jnp.concatenate(ones, axis=1), selector, NT, preferred_element_type=f32)
            for i, p in enumerate(pairs):
                count[p] += added[:, i * 256 : i * 256 + 256]
        return 0

    front, back = bounds[0], bounds[1]
    lower, upper = jnp.minimum(front, back), jnp.maximum(front, back)
    lax.fori_loop(0, lower, functools.partial(add, (0,)), 0)
    lax.fori_loop(lower, front, functools.partial(add, (0, 1)), 0)
    lax.fori_loop(upper, 64 // RANKS, functools.partial(add, (1,)), 0)
    for copy in copies:
        copy.wait()
    for x in range(4):
        lanes = slice((x % 2) * 128, (x % 2) * 128 + 128)
        if first:
            counts[x] = count[x // 2, :, lanes]
        rates = rates_of(x, now, below, beyond, metric, damping)
        for c in range(4):
            fringe = total[x // 2, c * 128 : c * 128 + 128, lanes]
            rate = rates[c] + fringe - counts[x] * now[c, x]
            if first:
                out[c, x] = now[c, x] + step_size * rate
                if x in (0, 3):
                    (low_plane if x == 0 else high_plane)[c] = out[c, x]
            else:
                out[c, x] = 0.5 * (held[5][c, x] + now[c, x]) + (0.5 * step_size) * rate


def deposit(first, arrived, *operands):
    fetched = operands[: 5 if first else 6]
    shape = fetched[0].shape
    if first:
        results = (
            jax.ShapeDtypeStruct((4, 128, 128), f32),
            jax.ShapeDtypeStruct((4, 128, 128), f32),
            jax.ShapeDtypeStruct(shape, f32),
            jax.ShapeDtypeStruct(shape[1:], f32),
            jax.ShapeDtypeStruct((2, 64, 128), i32),
            jax.ShapeDtypeStruct((2,), i32),
        )
        specs, result_specs = placed("vhhhhh"), tuple(placed("vvvvvs"))
    else:
        results, result_specs = jax.ShapeDtypeStruct(shape, f32), placed("v")[0]
        specs = placed("vhhhhhhvvs")
    return pl.pallas_call(
        functools.partial(deposit_kernel, first),
        out_shape=results,
        in_specs=specs,
        out_specs=result_specs,
        scratch_shapes=[
            pltpu.VMEM((8, 64, 128), f32),
            pltpu.VMEM((2, 512, 256), f32),
            pltpu.VMEM((2, 128, 256), f32),
            pltpu.SemaphoreType.DMA((len(fetched),)),
        ]
        + [pltpu.VMEM(operand.shape, f32) for operand in fetched],
        compiler_params=params(),
    )(arrived, *operands)


def neighbours(low_plane, high_plane):
    count = lax.axis_size("blk")
    forward = [(i, (i + 1) % count) for i in range(count)]
    backward = [((i + 1) % count, i) for i in range(count)]
    beyond = lax.ppermute(low_plane, "blk", backward)
    below = lax.ppermute(high_plane, "blk", forward)
    return below, beyond


def exchange(outgoing):
    return lax.all_to_all(outgoing, ("grid", "blk"), split_axis=0, concat_axis=0, tiled=True)


def local(state, metric, damping, donor, fractions, dest, recept):
    state, metric, damping = state[0], metric[0], damping[0]
    fractions = fractions.reshape(3, 1, -1)
    dest = dest.reshape(1, -1)
    below, beyond = neighbours(state[:, 0], state[:, 3])
    table, labels, tiles = prepare(donor, fractions, dest, recept)
    arrived = exchange(pack_rest(True, state, below, beyond, table, tiles, labels))
    low_plane, high_plane, section, *kept = deposit(True, arrived, state, below, beyond, metric, damping)
    below, beyond = neighbours(low_plane, high_plane)
    partial = pack_near(section, table, tiles)
    arrived = exchange(pack_rest(False, section, below, beyond, table, tiles, partial))
    return deposit(False, arrived, section, below, beyond, metric, damping, state, *kept)[None]


def solution(mesh):
    in_specs = (
        P("grid", None, "blk", None, None),
        P("grid", None, "blk", None, None),
        P("grid", "blk", None, None),
        P("grid", "blk"),
        P("grid", None, "blk"),
        P("grid", "blk", None),
        P("grid", "blk"),
    )
    out_specs = P("grid", None, "blk", None, None)
    return jax.shard_map(local, mesh=mesh, in_specs=in_specs, out_specs=out_specs, check_vma=False)
```

profile of v0, /device:TPU:1, one launch (start us, length us, event | category | flops | bytes accessed | tf_op | source)
XLA Modules:
  0.0 85.8 jit_solution(9371848457147832716)
XLA Ops:
  0.0 1.1 %slice_bitcast_fusion = (f32[4,128,128]{2,1,0:T(8,128)S(1)}, f32[4,128,128]{2,1,0:T(8,128)S(1)}) fusion(f32[4,4,128,128]{3,2,1,0:T(8,128)} %bitcast.12), kind=kLoop, calls=%fused_computation | loop fusion | bytes 1048576 | tf_op jit(solution)/shard_map/squeeze | solution.py:393
  1.1 1.5 %collective-permute-start.1 = (f32[4,128,128]{2,1,0:T(8,128)S(1)}, f32[4,128,128]{2,1,0:T(8,128)S(1)}, u32[]{:S(2)}, u32[]{:S(2)}) collective-permute-start(f32[4,128,128]{2,1,0:T(8,128)S(1)} %get-tuple-element.23), channel_id=1, source_target_pairs={{1,0},{2,1},{3,2},{4,3},{5,4},{6,5},{7,6},{8,7},{9,8},{10,9},{11,1... | collective-permute-start | bytes 786440 | tf_op jit(solution)/shard_map/ppermute | solution.py:380
  2.6 1.3 %collective-permute-start = (f32[4,128,128]{2,1,0:T(8,128)S(1)}, f32[4,128,128]{2,1,0:T(8,128)S(1)}, u32[]{:S(2)}, u32[]{:S(2)}) collective-permute-start(f32[4,128,128]{2,1,0:T(8,128)S(1)} %get-tuple-element.24), channel_id=1, source_target_pairs={{0,1},{1,2},{2,3},{3,4},{4,5},{5,6},{6,7},{7,8},{8,9},{9,10},{10,1... | collective-permute-start | bytes 786440 | tf_op jit(solution)/shard_map/ppermute | solution.py:381
  3.9 0.8 pad_add_fusion.numbers
  4.7 0.0 copy-start.3
  4.7 0.8 copy-done.3
  5.5 0.0 copy-start
  5.5 0.0 copy-start.2
  5.5 2.7 %shard_map.73 = (f32[7,24,256]{2,1,0:T(8,128)S(1)}, f32[128,128]{1,0:T(8,128)S(1)}, s32[4]{0:T(128)S(1)}) custom-call(s32[3,1,4096]{2,1,0:T(1,128)S(1)} %pad_add_fusion.numbers, f32[3,1,4096]{2,1,0:T(1,128)S(1)} %bitcast.20), custom_call_target="tpu_custom_call" | custom-call | flops 3000000000 | bytes 1000000 | tf_op jit(solution)/shard_map/pallas_call | solution.py:125
  8.2 0.0 copy-start.1
  8.2 0.0 collective-permute-done.1.refs_2_.refs_3_
  8.2 1.4 %collective-permute-done.refs_1_.refs_2_ = f32[4,128,128]{2,1,0:T(8,128)S(1)} collective-permute-done((f32[4,128,128]{2,1,0:T(8,128)S(1)}, f32[4,128,128]{2,1,0:T(8,128)S(1)}, u32[]{:S(2)}, u32[]{:S(2)}) %collective-permute-start) | collective-permute-done | bytes 262176 | tf_op jit(solution)/shard_map/ppermute | solution.py:381
  9.6 0.0 copy-done
  9.6 7.5 %shard_map.74 = f32[128,1,384]{2,1,0:T(1,128)S(1)} custom-call(f32[4,4,128,128]{3,2,1,0:T(8,128)S(1)} %bitcast.13, f32[4,128,128]{2,1,0:T(8,128)S(1)} %collective-permute-done.refs_1_.refs_2_, f32[4,128,128]{2,1,0:T(8,128)S(1)} %collective-permute-done.1.refs_2_.refs_3_, f32[7,24,256]{2,1,0:T(8,128)S(1)} %get-tuple-element.14.refs_3_.refs_1_, ...), custom_call_target="tpu_custom_call" | custom-call | tf_op jit(solution)/shard_map/pallas_call | solution.py:222
  17.1 22.2 %all_to_all.10.refs_0_ = f32[128,1,384]{2,1,0:T(1,128)S(1)} all-to-all(f32[128,1,384]{2,1,0:T(1,128)S(1)} %shard_map.74), channel_id=1, replica_groups=mesh['grid'=4,'blk'=32] {'grid','blk'}, dimensions={0} | all-to-all | bytes 393216 | tf_op jit(solution)/shard_map/all_to_all | solution.py:386
  39.3 0.0 copy-done.2
  39.3 0.0 copy-done.1
  39.3 8.3 %shard_map.75 = (f32[4,128,128]{2,1,0:T(8,128)S(1)}, f32[4,128,128]{2,1,0:T(8,128)S(1)}, f32[4,4,128,128]{3,2,1,0:T(8,128)S(1)}, f32[4,128,128]{2,1,0:T(8,128)S(...) custom-call(f32[128,1,384]{2,1,0:T(1,128)S(1)} %all_to_all.10.refs_0_, f32[4,4,128,128]{3,2,1,0:T(8,128)S(1)} %bitcast.14, ...), custom_call_target="tpu_custom_call" | custom-call | tf_op jit(solution)/shard_map/pallas_call | solution.py:360
  47.6 1.0 %collective-permute-start.2 = (f32[4,128,128]{2,1,0:T(8,128)S(1)}, f32[4,128,128]{2,1,0:T(8,128)S(1)}, u32[]{:S(2)}, u32[]{:S(2)}) collective-permute-start(f32[4,128,128]{2,1,0:T(8,128)S(1)} %get-tuple-element.18), channel_id=1, source_target_pairs={{0,1},{1,2},{2,3},{3,4},{4,5},{5,6},{6,7},{7,8},{8,9},{9,10},{10,1... | collective-permute-start | bytes 786440 | tf_op jit(solution)/shard_map/ppermute | solution.py:381
  48.6 0.0 collective-permute-start.3
  48.6 6.1 %shard_map.76.refs_5_ = f32[128,512]{1,0:T(8,128)S(1)} custom-call(f32[4,4,128,128]{3,2,1,0:T(8,128)S(1)} %get-tuple-element.17.refs_0_.refs_1_, f32[7,24,256]{2,1,0:T(8,128)S(1)} %get-tuple-element.14.refs_3_.refs_1_, s32[4]{0:T(128)S(1)} %get-tuple-element.15.refs_4_.refs_2_), custom_call_target="tpu_custom_call" | custom-call | flops 5000000000 | bytes 1000000 | tf_op jit(solution)/shard_map/pallas_call | solution.py:205
  54.7 0.0 collective-permute-done.2.refs_1_.refs_2_
  54.7 0.0 collective-permute-done.3.refs_2_.refs_3_
  54.7 3.3 %shard_map.77 = f32[128,1,256]{2,1,0:T(1,128)S(1)} custom-call(f32[4,4,128,128]{3,2,1,0:T(8,128)S(1)} %get-tuple-element.17.refs_0_.refs_1_, f32[4,128,128]{2,1,0:T(8,128)S(1)} %collective-permute-done.2.refs_1_.refs_2_, f32[4,128,128]{2,1,0:T(8,128)S(1)} %collective-permute-done.3.refs_2_.refs_3_, f32[7,24,256]{2,1,0:T(8,128)S(1)} %get-tuple-element.14.refs_3_.refs_1_, ...), custom_call_target="tpu_custom_call" | custom-call | tf_op jit(solution)/shard_map/pallas_call | solution.py:222
  58.0 19.2 %all_to_all.11.refs_0_ = f32[128,1,256]{2,1,0:T(1,128)S(1)} all-to-all(f32[128,1,256]{2,1,0:T(1,128)S(1)} %shard_map.77), channel_id=1, replica_groups=mesh['grid'=4,'blk'=32] {'grid','blk'}, dimensions={0} | all-to-all | bytes 262144 | tf_op jit(solution)/shard_map/all_to_all | solution.py:386
  77.2 8.4 %shard_map.78 = f32[4,4,128,128]{3,2,1,0:T(8,128)} custom-call(f32[128,1,256]{2,1,0:T(1,128)S(1)} %all_to_all.11.refs_0_, f32[4,4,128,128]{3,2,1,0:T(8,128)S(1)} %get-tuple-element.17.refs_0_.refs_1_, f32[4,128,128]{2,1,0:T(8,128)S(1)} %collective-permute-done.2.refs_1_.refs_2_, f32[4,128,128]{2,1,0:T(8,128)S(1)} %collective-permute-done.3.refs_2_.refs_3_, ...), custom_call_target="tpu_custom_call" | custom-call | tf_op jit(solution)/shard_map/pallas_call | solution.py:360
Async XLA Ops:
  1.1 7.1 %collective-permute-start.1 = (f32[4,128,128]{2,1,0:T(8,128)S(1)}, f32[4,128,128]{2,1,0:T(8,128)S(1)}, u32[]{:S(2)}, u32[]{:S(2)}) collective-permute-start(f32[4,128,128]{2,1,0:T(8,128)S(1)} %get-tuple-element.23), channel_id=1, source_target_pairs={{1,0},{2,1},{3,2},{4,3},{5,4},{6,5},{7,6},{8,7},{9,8},{10,9},{11,1... | collective-permute-start | bytes 786440 | tf_op jit(solution)/shard_map/ppermute | solution.py:380
  2.6 7.0 %collective-permute-start = (f32[4,128,128]{2,1,0:T(8,128)S(1)}, f32[4,128,128]{2,1,0:T(8,128)S(1)}, u32[]{:S(2)}, u32[]{:S(2)}) collective-permute-start(f32[4,128,128]{2,1,0:T(8,128)S(1)} %get-tuple-element.24), channel_id=1, source_target_pairs={{0,1},{1,2},{2,3},{3,4},{4,5},{5,6},{6,7},{7,8},{8,9},{9,10},{10,1... | collective-permute-start | bytes 786440 | tf_op jit(solution)/shard_map/ppermute | solution.py:381
  4.7 0.8 copy-start.3
  5.5 4.1 %copy-start = (f32[1,4,4,128,128]{4,3,2,1,0:T(8,128)S(1)}, f32[1,4,4,128,128]{4,3,2,1,0:T(8,128)}, u32[]{:S(2)}) copy-start(f32[1,4,4,128,128]{4,3,2,1,0:T(8,128)} %param.7) | copy-start | bytes 3145732
  5.5 33.9 %copy-start.2 = (f32[1,4,128,128]{3,2,1,0:T(8,128)S(1)}, f32[1,4,128,128]{3,2,1,0:T(8,128)}, u32[]{:S(2)}) copy-start(f32[1,4,128,128]{3,2,1,0:T(8,128)} %param.9) | copy-start | bytes 786436
  8.2 31.1 %copy-start.1 = (f32[1,9,4,128,128]{4,3,2,1,0:T(8,128)S(1)}, f32[1,9,4,128,128]{4,3,2,1,0:T(8,128)}, u32[]{:S(2)}) copy-start(f32[1,9,4,128,128]{4,3,2,1,0:T(8,128)} %param.8) | copy-start | bytes 7077892
  47.6 7.1 %collective-permute-start.2 = (f32[4,128,128]{2,1,0:T(8,128)S(1)}, f32[4,128,128]{2,1,0:T(8,128)S(1)}, u32[]{:S(2)}, u32[]{:S(2)}) collective-permute-start(f32[4,128,128]{2,1,0:T(8,128)S(1)} %get-tuple-element.18), channel_id=1, source_target_pairs={{0,1},{1,2},{2,3},{3,4},{4,5},{5,6},{6,7},{7,8},{8,9},{9,10},{10,1... | collective-permute-start | bytes 786440 | tf_op jit(solution)/shard_map/ppermute | solution.py:381
  48.6 6.1 %collective-permute-start.3 = (f32[4,128,128]{2,1,0:T(8,128)S(1)}, f32[4,128,128]{2,1,0:T(8,128)S(1)}, u32[]{:S(2)}, u32[]{:S(2)}) collective-permute-start(f32[4,128,128]{2,1,0:T(8,128)S(1)} %get-tuple-element.19), channel_id=1, source_target_pairs={{1,0},{2,1},{3,2},{4,3},{5,4},{6,5},{7,6},{8,7},{9,8},{10,9},{11,1... | collective-permute-start | bytes 786440 | tf_op jit(solution)/shard_map/ppermute | solution.py:380
where the time goes:
time: 86.3 us; the launch traced here: 85.8 us
  blocking collectives  41.4 us (48%)
  Pallas kernels  36.3 us (42%)
  starting transfers between devices  3.85 us (4%)
  local copies, waits for them, and re-layouts  1.88 us (2%)
  waiting for transfers between devices  1.4 us (2%)
    all_to_all x2, blocking collectives, exchange(): lax.all_to_all(outgoing, ('grid', 'blk'), split_axis=0, concat_axis=0, ti...  41.4 us
    pallas_call x2, Pallas kernels, deposit(): pl.pallas_call(functools.partial(deposit_kernel, first), out_shape=result...  16.7 us
    pallas_call x2, Pallas kernels, pack_rest(): pl.pallas_call(functools.partial(pack_kernel, 1, first), out_shape=jax.Sh...  10.8 us
    pallas_call x1, Pallas kernels, pack_near(): pl.pallas_call(functools.partial(pack_kernel, 0, False), out_shape=jax.Sh...  6.07 us
    pallas_call x1, Pallas kernels, prepare(): pl.pallas_call(prepare_kernel, out_shape=(jax.ShapeDtypeStruct((7, DONOR_...  2.71 us
    ppermute x2, starting transfers between devices, neighbours(): below = lax.ppermute(high_plane, 'blk', forward)  2.35 us
  transfers between devices with their start and end apart: 4, of which 1 were waited for; matrix products, arithmetic and copies ran while one was open for 1% of the time, Pallas kernels for 10%

commit v1 on v0

--- a/solution.py
+++ b/solution.py
@@ -29,7 +29,7 @@
 TILE = 256
 NEAR_GROUP = 8
 FAR_GROUP = 5
-WHOLE_GROUP = 10
+WHOLE_GROUP = 20
 DONOR_ROWS = 24
 RANKS = 16
 

time: 86.3 us -> 88.4 us (1.024); the launches traced: 85.8 us -> 89.5 us
  Pallas kernels: 36.3 us -> 41.3 us
  blocking collectives: 41.4 us -> 40.1 us
    pallas_call x2, Pallas kernels: 16.7 us -> 21.9 us  [deposit(): pl.pallas_call(functools.partial(deposit_kernel, first), out_shape=result...]
    all_to_all x2, blocking collectives: 41.4 us -> 40.1 us  [exchange(): lax.all_to_all(outgoing, ('grid', 'blk'), split_axis=0, concat_axis=0, ti...]
    ppermute x2, starting transfers between devices: 2.35 us -> 1.42 us  [neighbours(): below = lax.ppermute(high_plane, 'blk', forward)]
where the time goes in v1:
time: 88.4 us; the launch traced here: 89.5 us
  Pallas kernels  41.3 us (47%)
  blocking collectives  40.1 us (45%)
  starting transfers between devices  3.7 us (4%)
  local copies, waits for them, and re-layouts  1.88 us (2%)
  waiting for transfers between devices  1.4 us (2%)
    all_to_all x2, blocking collectives, exchange(): lax.all_to_all(outgoing, ('grid', 'blk'), split_axis=0, concat_axis=0, ti...  40.1 us
    pallas_call x2, Pallas kernels, deposit(): pl.pallas_call(functools.partial(deposit_kernel, first), out_shape=result...  21.9 us
    pallas_call x2, Pallas kernels, pack_rest(): pl.pallas_call(functools.partial(pack_kernel, 1, first), out_shape=jax.Sh...  10.6 us
    pallas_call x1, Pallas kernels, pack_near(): pl.pallas_call(functools.partial(pack_kernel, 0, False), out_shape=jax.Sh...  6.08 us
    pallas_call x1, Pallas kernels, prepare(): pl.pallas_call(prepare_kernel, out_shape=(jax.ShapeDtypeStruct((7, DONOR_...  2.71 us
    ppermute x2, starting transfers between devices, neighbours(): beyond = lax.ppermute(low_plane, 'blk', backward)  2.28 us
  transfers between devices with their start and end apart: 4, of which 1 were waited for; matrix products, arithmetic and copies ran while one was open for 1% of the time, Pallas kernels for 10%

profile of v1, /device:TPU:1, one launch (start us, length us, event | category | flops | bytes accessed | tf_op | source)
XLA Modules:
  0.0 89.5 jit_solution(6824789936533748868)
XLA Ops:
  0.0 1.1 %slice_bitcast_fusion = (f32[4,128,128]{2,1,0:T(8,128)S(1)}, f32[4,128,128]{2,1,0:T(8,128)S(1)}) fusion(f32[4,4,128,128]{3,2,1,0:T(8,128)} %bitcast.12), kind=kLoop, calls=%fused_computation | loop fusion | bytes 1048576 | tf_op jit(solution)/shard_map/squeeze | solution.py:393
  1.1 1.5 %collective-permute-start.1 = (f32[4,128,128]{2,1,0:T(8,128)S(1)}, f32[4,128,128]{2,1,0:T(8,128)S(1)}, u32[]{:S(2)}, u32[]{:S(2)}) collective-permute-start(f32[4,128,128]{2,1,0:T(8,128)S(1)} %get-tuple-element.23), channel_id=1, source_target_pairs={{1,0},{2,1},{3,2},{4,3},{5,4},{6,5},{7,6},{8,7},{9,8},{10,9},{11,1... | collective-permute-start | bytes 786440 | tf_op jit(solution)/shard_map/ppermute | solution.py:380
  2.6 1.3 %collective-permute-start = (f32[4,128,128]{2,1,0:T(8,128)S(1)}, f32[4,128,128]{2,1,0:T(8,128)S(1)}, u32[]{:S(2)}, u32[]{:S(2)}) collective-permute-start(f32[4,128,128]{2,1,0:T(8,128)S(1)} %get-tuple-element.24), channel_id=1, source_target_pairs={{0,1},{1,2},{2,3},{3,4},{4,5},{5,6},{6,7},{7,8},{8,9},{9,10},{10,1... | collective-permute-start | bytes 786440 | tf_op jit(solution)/shard_map/ppermute | solution.py:381
  3.9 0.8 pad_add_fusion.numbers
  4.7 0.0 copy-start.3
  4.7 0.8 copy-done.3
  5.5 0.0 copy-start
  5.5 0.0 copy-start.2
  5.5 2.7 %shard_map.73 = (f32[7,24,256]{2,1,0:T(8,128)S(1)}, f32[128,128]{1,0:T(8,128)S(1)}, s32[4]{0:T(128)S(1)}) custom-call(s32[3,1,4096]{2,1,0:T(1,128)S(1)} %pad_add_fusion.numbers, f32[3,1,4096]{2,1,0:T(1,128)S(1)} %bitcast.20), custom_call_target="tpu_custom_call" | custom-call | flops 3000000000 | bytes 1000000 | tf_op jit(solution)/shard_map/pallas_call | solution.py:125
  8.2 0.0 copy-start.1
  8.2 0.0 collective-permute-done.1.refs_2_.refs_3_
  8.2 1.4 %collective-permute-done.refs_1_.refs_2_ = f32[4,128,128]{2,1,0:T(8,128)S(1)} collective-permute-done((f32[4,128,128]{2,1,0:T(8,128)S(1)}, f32[4,128,128]{2,1,0:T(8,128)S(1)}, u32[]{:S(2)}, u32[]{:S(2)}) %collective-permute-start) | collective-permute-done | bytes 262176 | tf_op jit(solution)/shard_map/ppermute | solution.py:381
  9.6 0.0 copy-done
  9.6 7.4 %shard_map.74 = f32[128,1,384]{2,1,0:T(1,128)S(1)} custom-call(f32[4,4,128,128]{3,2,1,0:T(8,128)S(1)} %bitcast.13, f32[4,128,128]{2,1,0:T(8,128)S(1)} %collective-permute-done.refs_1_.refs_2_, f32[4,128,128]{2,1,0:T(8,128)S(1)} %collective-permute-done.1.refs_2_.refs_3_, f32[7,24,256]{2,1,0:T(8,128)S(1)} %get-tuple-element.14.refs_3_.refs_1_, ...), custom_call_target="tpu_custom_call" | custom-call | tf_op jit(solution)/shard_map/pallas_call | solution.py:222
  17.0 22.2 %all_to_all.10.refs_0_ = f32[128,1,384]{2,1,0:T(1,128)S(1)} all-to-all(f32[128,1,384]{2,1,0:T(1,128)S(1)} %shard_map.74), channel_id=1, replica_groups=mesh['grid'=4,'blk'=32] {'grid','blk'}, dimensions={0} | all-to-all | bytes 393216 | tf_op jit(solution)/shard_map/all_to_all | solution.py:386
  39.2 0.0 copy-done.2
  39.2 0.0 copy-done.1
  39.2 11.1 %shard_map.75 = (f32[4,128,128]{2,1,0:T(8,128)S(1)}, f32[4,128,128]{2,1,0:T(8,128)S(1)}, f32[4,4,128,128]{3,2,1,0:T(8,128)S(1)}, f32[4,128,128]{2,1,0:T(8,128)S(...) custom-call(f32[128,1,384]{2,1,0:T(1,128)S(1)} %all_to_all.10.refs_0_, f32[4,4,128,128]{3,2,1,0:T(8,128)S(1)} %bitcast.14, ...), custom_call_target="tpu_custom_call" | custom-call | tf_op jit(solution)/shard_map/pallas_call | solution.py:360
  50.3 0.1 collective-permute-start.2
  50.4 0.8 collective-permute-start.3
  51.1 6.1 %shard_map.76.refs_5_ = f32[128,512]{1,0:T(8,128)S(1)} custom-call(f32[4,4,128,128]{3,2,1,0:T(8,128)S(1)} %get-tuple-element.17.refs_0_.refs_1_, f32[7,24,256]{2,1,0:T(8,128)S(1)} %get-tuple-element.14.refs_3_.refs_1_, s32[4]{0:T(128)S(1)} %get-tuple-element.15.refs_4_.refs_2_), custom_call_target="tpu_custom_call" | custom-call | flops 5000000000 | bytes 1000000 | tf_op jit(solution)/shard_map/pallas_call | solution.py:205
  57.2 0.0 collective-permute-done.2.refs_1_.refs_2_
  57.2 0.0 collective-permute-done.3.refs_2_.refs_3_
  57.3 3.3 %shard_map.77 = f32[128,1,256]{2,1,0:T(1,128)S(1)} custom-call(f32[4,4,128,128]{3,2,1,0:T(8,128)S(1)} %get-tuple-element.17.refs_0_.refs_1_, f32[4,128,128]{2,1,0:T(8,128)S(1)} %collective-permute-done.2.refs_1_.refs_2_, f32[4,128,128]{2,1,0:T(8,128)S(1)} %collective-permute-done.3.refs_2_.refs_3_, f32[7,24,256]{2,1,0:T(8,128)S(1)} %get-tuple-element.14.refs_3_.refs_1_, ...), custom_call_target="tpu_custom_call" | custom-call | tf_op jit(solution)/shard_map/pallas_call | solution.py:222
  60.5 17.9 %all_to_all.11.refs_0_ = f32[128,1,256]{2,1,0:T(1,128)S(1)} all-to-all(f32[128,1,256]{2,1,0:T(1,128)S(1)} %shard_map.77), channel_id=1, replica_groups=mesh['grid'=4,'blk'=32] {'grid','blk'}, dimensions={0} | all-to-all | bytes 262144 | tf_op jit(solution)/shard_map/all_to_all | solution.py:386
  78.4 10.8 %shard_map.78 = f32[4,4,128,128]{3,2,1,0:T(8,128)} custom-call(f32[128,1,256]{2,1,0:T(1,128)S(1)} %all_to_all.11.refs_0_, f32[4,4,128,128]{3,2,1,0:T(8,128)S(1)} %get-tuple-element.17.refs_0_.refs_1_, f32[4,128,128]{2,1,0:T(8,128)S(1)} %collective-permute-done.2.refs_1_.refs_2_, f32[4,128,128]{2,1,0:T(8,128)S(1)} %collective-permute-done.3.refs_2_.refs_3_, ...), custom_call_target="tpu_custom_call" | custom-call | tf_op jit(solution)/shard_map/pallas_call | solution.py:360
Async XLA Ops:
  1.1 7.1 %collective-permute-start.1 = (f32[4,128,128]{2,1,0:T(8,128)S(1)}, f32[4,128,128]{2,1,0:T(8,128)S(1)}, u32[]{:S(2)}, u32[]{:S(2)}) collective-permute-start(f32[4,128,128]{2,1,0:T(8,128)S(1)} %get-tuple-element.23), channel_id=1, source_target_pairs={{1,0},{2,1},{3,2},{4,3},{5,4},{6,5},{7,6},{8,7},{9,8},{10,9},{11,1... | collective-permute-start | bytes 786440 | tf_op jit(solution)/shard_map/ppermute | solution.py:380
  2.6 7.0 %collective-permute-start = (f32[4,128,128]{2,1,0:T(8,128)S(1)}, f32[4,128,128]{2,1,0:T(8,128)S(1)}, u32[]{:S(2)}, u32[]{:S(2)}) collective-permute-start(f32[4,128,128]{2,1,0:T(8,128)S(1)} %get-tuple-element.24), channel_id=1, source_target_pairs={{0,1},{1,2},{2,3},{3,4},{4,5},{5,6},{6,7},{7,8},{8,9},{9,10},{10,1... | collective-permute-start | bytes 786440 | tf_op jit(solution)/shard_map/ppermute | solution.py:381
  4.7 0.8 copy-start.3
  5.5 4.1 %copy-start = (f32[1,4,4,128,128]{4,3,2,1,0:T(8,128)S(1)}, f32[1,4,4,128,128]{4,3,2,1,0:T(8,128)}, u32[]{:S(2)}) copy-start(f32[1,4,4,128,128]{4,3,2,1,0:T(8,128)} %param.7) | copy-start | bytes 3145732
  5.5 33.7 %copy-start.2 = (f32[1,4,128,128]{3,2,1,0:T(8,128)S(1)}, f32[1,4,128,128]{3,2,1,0:T(8,128)}, u32[]{:S(2)}) copy-start(f32[1,4,128,128]{3,2,1,0:T(8,128)} %param.9) | copy-start | bytes 786436
  8.2 31.0 %copy-start.1 = (f32[1,9,4,128,128]{4,3,2,1,0:T(8,128)S(1)}, f32[1,9,4,128,128]{4,3,2,1,0:T(8,128)}, u32[]{:S(2)}) copy-start(f32[1,9,4,128,128]{4,3,2,1,0:T(8,128)} %param.8) | copy-start | bytes 7077892
  50.3 7.0 %collective-permute-start.2 = (f32[4,128,128]{2,1,0:T(8,128)S(1)}, f32[4,128,128]{2,1,0:T(8,128)S(1)}, u32[]{:S(2)}, u32[]{:S(2)}) collective-permute-start(f32[4,128,128]{2,1,0:T(8,128)S(1)} %get-tuple-element.18), channel_id=1, source_target_pairs={{0,1},{1,2},{2,3},{3,4},{4,5},{5,6},{6,7},{7,8},{8,9},{9,10},{10,1... | collective-permute-start | bytes 786440 | tf_op jit(solution)/shard_map/ppermute | solution.py:381
  50.4 6.9 %collective-permute-start.3 = (f32[4,128,128]{2,1,0:T(8,128)S(1)}, f32[4,128,128]{2,1,0:T(8,128)S(1)}, u32[]{:S(2)}, u32[]{:S(2)}) collective-permute-start(f32[4,128,128]{2,1,0:T(8,128)S(1)} %get-tuple-element.19), channel_id=1, source_target_pairs={{1,0},{2,1},{3,2},{4,3},{5,4},{6,5},{7,6},{8,7},{9,8},{10,9},{11,1... | collective-permute-start | bytes 786440 | tf_op jit(solution)/shard_map/ppermute | solution.py:380
